TPU v7x, 32 devices: a whole 2x2x4 slice. The times are simulated.
32 devices in a mesh: groups: 2 (over y), row: 4 (over z), col: 4 (over x, core).
Axes of the slice: x: 2, y: 2, z: 4, core: 2. Of those that a mesh axis runs over, the one named last changes fastest.
Arguments:
- tokens: bfloat16 [1024, 4096], P(('groups', 'row'), 'col'), parts along dimension 0, may hold values from -90 to 90
- norm_gain: float32 [4096], P('col'), may hold values from 0.5 to 1.5
- gate_weight: bfloat16 [4096, 16384], P('col', 'row'), may hold values from -0.09375 to 0.09375
- up_weight: bfloat16 [4096, 16384], P('col', 'row'), may hold values from -0.09375 to 0.09375
- down_weight: bfloat16 [16384, 4096], P('row', 'col'), may hold values from -0.046875 to 0.046875
Outputs:
- block_out: bfloat16 [1024, 4096], P(('groups', 'row'), 'col'), parts along dimension 0
There are 2 independent parts, one for each index of `groups`. A program takes and returns all parts, laid end to end along the dimension named above; an argument that names none is the same for every part. Nothing has to cross between parts.
All inputs are finite; a program needn't handle non-finite values.
Results may differ from a plain program's by a relative error of at most 0.02.
Values may be sent and summed in bfloat16 or wider, within the bound.
A program may use at most 128 MiB of HBM per device.

v0:
```python
import jax
import jax.numpy as jnp
from jax import lax
from jax.sharding import PartitionSpec as P

epsilon = 1e-05


def normalize(source, total_squares, width_total, norm_gain):
    inverse_rms = lax.rsqrt(total_squares / width_total + epsilon)
    return (source.astype(jnp.float32) * inverse_rms[:, None] * norm_gain[None, :]).astype(
        jnp.bfloat16
    )


def per_device(tokens, norm_gain, gate_weight, up_weight, down_weight):
    width_total = tokens.shape[1] * lax.axis_size("col")
    split_at = gate_weight.shape[1]
    both_weights = jnp.concatenate([gate_weight, up_weight], axis=1)
    local_squares = jnp.sum(jnp.square(tokens.astype(jnp.float32)), axis=1)
    total_squares = lax.psum(local_squares, "col")
    normed = normalize(tokens, total_squares, width_total, norm_gain)
    gathered = lax.all_gather(normed, "row", axis=0, tiled=True)
    block_rows = gathered
    summed = lax.psum_scatter(
        jnp.dot(block_rows, both_weights, preferred_element_type=jnp.float32).astype(jnp.bfloat16),
        "col",
        scatter_dimension=0,
        tiled=True,
    ).astype(jnp.float32)
    hidden_part = (jax.nn.silu(summed[:, :split_at]) * summed[:, split_at:]).astype(jnp.bfloat16)
    hidden = lax.all_gather(hidden_part, "col", axis=0, tiled=True)
    block_rows = hidden
    return lax.psum_scatter(
        jnp.dot(block_rows, down_weight, preferred_element_type=jnp.float32).astype(jnp.bfloat16),
        "row",
        scatter_dimension=0,
        tiled=True,
    )


def solution(mesh):
    placed = (
        P(("groups", "row"), "col"),
        P("col"),
        P("col", "row"),
        P("col", "row"),
        P("row", "col"),
    )
    return jax.shard_map(
        per_device,
        mesh=mesh,
        in_specs=placed,
        out_specs=P(("groups", "row"), "col"),
        check_vma=False,
    )
```

profile of v0, /device:TPU:0, one launch (start us, length us, event | category | flops | bytes accessed | tf_op | source)
XLA Modules:
  0.0 214.6 jit_solution(8213113644927217040)
XLA Ops:
  6.5 0.0 all-gather.3.cloned.1.call-start
  6.5 1.1 fusion.8
  7.6 8.3 %psum.7 = f32[128]{0:T(128)S(1)} all-reduce(f32[128]{0:T(128)S(1)} %fusion.8), channel_id=1, replica_groups=mesh['groups'=2,'row'=4,'col'=4] {'col'}, use_global_device_ids=true, to_apply=%region_1.0 | all-reduce | flops 128 | bytes 1024 | tf_op jit(solution)/shard_map/psum | solution.py:21
  16.0 1.8 fusion.10
  17.8 0.0 all-gather.3.cloned.1.call-update
  17.8 0.0 reduce-scatter.3.cloned.1.call-start
  17.8 28.4 %all-gather.3.cloned.1.call-done = bf16[512,1024]{1,0:T(8,128)(2,1)} async-done(((bf16[128,1024]{1,0:T(8,128)(2,1)}), bf16[512,1024]{1,0:T(8,128)(2,1)}) %all-gather.3.cloned.1.call-update) | async-done | bytes 1048592 | tf_op jit(solution)/shard_map/all_gather | solution.py:23
  46.2 14.8 %fusion.4 = bf16[512,8192]{1,0:T(8,128)(2,1)} fusion(bf16[512,1024]{1,0:T(8,128)(2,1)} %all-gather.3.cloned.1.call-done, bf16[1024,4096]{1,0:T(8,128)(2,1)} %param.8, bf16[1024,4096]{1,0:T(8,128)(2,1)} %param.7), kind=kOutput, calls=%fused_computation.4 | convolution fusion | flops 8627683328 | bytes 26214400 | tf_op jit(solution)/shard_map/dot_general | solution.py:26
  61.0 0.0 reduce-scatter.3.cloned.1.call-update
  61.0 0.0 all-gather.5.cloned.1.call-start
  61.0 71.3 %reduce-scatter.3.cloned.1.call-done = bf16[128,8192]{1,0:T(8,128)(2,1)} async-done(((bf16[512,8192]{1,0:T(8,128)(2,1)}), bf16[128,8192]{1,0:T(8,128)(2,1)}) %reduce-scatter.3.cloned.1.call-update) | async-done | bytes 2097168 | tf_op jit(solution)/shard_map/reduce_scatter | solution.py:25
  132.4 2.0 convert_element_type.22
  134.4 1.5 fusion.7
  135.9 0.0 all-gather.5.cloned.1.call-update
  135.9 0.0 reduce-scatter.5.cloned.1.call-start
  136.0 34.6 %all-gather.5.cloned.1.call-done = bf16[512,4096]{1,0:T(8,128)(2,1)} async-done(((bf16[128,4096]{1,0:T(8,128)(2,1)}), bf16[512,4096]{1,0:T(8,128)(2,1)}) %all-gather.5.cloned.1.call-update) | async-done | bytes 4194320 | tf_op jit(solution)/shard_map/all_gather | solution.py:32
  170.6 10.1 %convolution_convert_fusion = bf16[512,1024]{1,0:T(8,128)(2,1)} fusion(bf16[512,4096]{1,0:T(8,128)(2,1)} %all-gather.5.cloned.1.call-done, bf16[4096,1024]{1,0:T(8,128)(2,1)} %param.9), kind=kOutput, calls=%fused_computation.7 | convolution fusion | flops 4295491584 | bytes 13631488 | tf_op jit(solution)/shard_map/dot_general | solution.py:35
  180.7 0.0 reduce-scatter.5.cloned.1.call-update
  180.7 27.3 %reduce-scatter.5.cloned.1.call-done = bf16[128,1024]{1,0:T(8,128)(2,1)} async-done(((bf16[512,1024]{1,0:T(8,128)(2,1)}), bf16[128,1024]{1,0:T(8,128)(2,1)}) %reduce-scatter.5.cloned.1.call-update) | async-done | bytes 262160 | tf_op jit(solution)/shard_map/reduce_scatter | solution.py:34
  (1 shorter events, 0.0 us)
Async XLA Ops:
  6.5 39.7 %all-gather.3.cloned.1.call-start = ((), (), s32[]{:S(2)}) async-start(), calls=%async_computation.2 | async-start | bytes 1310720 | tf_op jit(solution)/shard_map/all_gather | solution.py:23
  17.8 114.6 %reduce-scatter.3.cloned.1.call-start = ((), (), s32[]{:S(2)}) async-start(), calls=%async_computation.3 | async-start | bytes 10485760 | tf_op jit(solution)/shard_map/reduce_scatter | solution.py:25
  61.0 109.6 %all-gather.5.cloned.1.call-start = ((), (), s32[]{:S(2)}) async-start(), calls=%async_computation.4 | async-start | bytes 5242880 | tf_op jit(solution)/shard_map/all_gather | solution.py:32
  135.9 72.1 %reduce-scatter.5.cloned.1.call-start = ((), (), s32[]{:S(2)}) async-start(), calls=%async_computation.5 | async-start | bytes 1310720 | tf_op jit(solution)/shard_map/reduce_scatter | solution.py:34
Sparse Core Ops, SparseCore 0:
  17.9 28.2 all-gather.2
  61.1 71.2 reduce-scatter.2
  136.1 34.4 all-gather.4
  180.9 27.1 reduce-scatter.4
where the time goes:
time: 215 us
  waiting for transfers between devices  162 us (75%)
  matrix products  24.9 us (12%)
  between operations  13.1 us (6%)
  blocking collectives  8.34 us (4%)
  other arithmetic  6.43 us (3%)
    reduce_scatter x1, waiting for transfers between devices, per_device(): lax.psum_scatter(jnp.dot(block_rows, both_weights, preferred_element_type...  71.3 us
    all_gather x1, waiting for transfers between devices, per_device(): hidden = lax.all_gather(hidden_part, 'col', axis=0, tiled=True)  34.6 us
    all_gather x1, waiting for transfers between devices, per_device(): gathered = lax.all_gather(normed, 'row', axis=0, tiled=True)  28.4 us
    reduce_scatter x1, waiting for transfers between devices, per_device(): lax.psum_scatter(jnp.dot(block_rows, down_weight, preferred_element_type=...  27.3 us
    dot_general x1, matrix products, per_device(): jnp.dot(block_rows, both_weights, preferred_element_type=jnp.float32)  14.8 us
    dot_general x1, matrix products, per_device(): jnp.dot(block_rows, down_weight, preferred_element_type=jnp.float32)  10.1 us
    psum x1, blocking collectives, per_device(): total_squares = lax.psum(local_squares, 'col')  8.34 us
  transfers between devices with their start and end apart: 4, of which 4 were waited for; matrix products, arithmetic and copies ran while one was open for 0% of the time, Pallas kernels for 0%

commit v1 on v0

--- a/solution.py
+++ b/solution.py
@@ -20,7 +20,16 @@
     local_squares = jnp.sum(jnp.square(tokens.astype(jnp.float32)), axis=1)
     total_squares = lax.psum(local_squares, "col")
     normed = normalize(tokens, total_squares, width_total, norm_gain)
-    gathered = lax.all_gather(normed, "row", axis=0, tiled=True)
+    count_all = lax.psum(1, axis_name="row")
+    chunks = [(dev, (dev + 1) % count_all) for dev in range(count_all)]
+    frames = [(dev, (dev - 1) % count_all) for dev in range(count_all)]
+    work_now, side_arr = ([normed], [normed])
+    for _ in range(count_all // 2):
+        work_now.append(lax.ppermute(work_now[-1], axis_name="row", perm=chunks))
+    for _ in range((count_all - 1) // 2):
+        side_arr.append(lax.ppermute(side_arr[-1], axis_name="row", perm=frames))
+    res = jnp.concatenate([*work_now[::-1], *side_arr[1:]], axis=0)
+    gathered = jnp.roll(res, (lax.axis_index("row") - count_all // 2) * normed.shape[0], axis=0)
     block_rows = gathered
     summed = lax.psum_scatter(
         jnp.dot(block_rows, both_weights, preferred_element_type=jnp.float32).astype(jnp.bfloat16),

time: 215 us -> 208 us (0.967)
  waiting for transfers between devices: 162 us -> 149 us
  starting transfers between devices: 0.13 us -> 5.54 us
    all_gather x1 -> x0, waiting for transfers between devices: 28.4 us -> none  [per_device(): gathered = lax.all_gather(normed, 'row', axis=0, tiled=True)]
    ppermute x0 -> x3, waiting for transfers between devices: none -> 14 us  [the longest x2 14 us: per_device(): work_now.append(lax.ppermute(work_now[-1], axis_name='row', perm=chunks))]
    ppermute x0 -> x3, starting transfers between devices: none -> 5.45 us  [the longest x1 3.82 us: per_device(): side_arr.append(lax.ppermute(side_arr[-1], axis_name='row', perm=frames))]
  transfers between devices with their start and end apart: 4 -> 6, of which waited for: 4 -> 5; matrix products, arithmetic and copies ran while one was open for 0% -> 1% of each run, Pallas kernels for 0% -> 0%
where the time goes in v1:
time: 208 us
  waiting for transfers between devices  149 us (72%)
  matrix products  24.7 us (12%)
  between operations  13.2 us (6%)
  blocking collectives  8.34 us (4%)
  other arithmetic  7.03 us (3%)
  starting transfers between devices  5.54 us (3%)
    reduce_scatter x1, waiting for transfers between devices, per_device(): lax.psum_scatter(jnp.dot(block_rows, both_weights, preferred_element_type...  72.7 us
    all_gather x1, waiting for transfers between devices, per_device(): hidden = lax.all_gather(hidden_part, 'col', axis=0, tiled=True)  34.6 us
    reduce_scatter x1, waiting for transfers between devices, per_device(): lax.psum_scatter(jnp.dot(block_rows, down_weight, preferred_element_type=...  27.3 us
    dot_general x1, matrix products, per_device(): jnp.dot(block_rows, both_weights, preferred_element_type=jnp.float32)  14.6 us
    ppermute x2, waiting for transfers between devices, per_device(): work_now.append(lax.ppermute(work_now[-1], axis_name='row', perm=chunks))  14 us
    dot_general x1, matrix products, per_device(): jnp.dot(block_rows, down_weight, preferred_element_type=jnp.float32)  10.1 us
    psum x1, blocking collectives, per_device(): total_squares = lax.psum(local_squares, 'col')  8.34 us
  transfers between devices with their start and end apart: 6, of which 5 were waited for; matrix products, arithmetic and copies ran while one was open for 1% of the time, Pallas kernels for 0%

profile of v1, /device:TPU:0, one launch (start us, length us, event | category | flops | bytes accessed | tf_op | source)
XLA Modules:
  0.0 207.6 jit_solution(2819930543322083823)
XLA Ops:
  6.5 0.0 copy-start
  6.5 0.0 copy-start.1
  6.5 0.0 reduce-scatter.3.cloned.1.call-start
  6.5 1.1 fusion.9
  7.7 8.3 %psum.7 = f32[128]{0:T(128)S(1)} all-reduce(f32[128]{0:T(128)S(1)} %fusion.9), channel_id=1, replica_groups=mesh['groups'=2,'row'=4,'col'=4] {'col'}, use_global_device_ids=true, to_apply=%region_1.0 | all-reduce | flops 128 | bytes 1024 | tf_op jit(solution)/shard_map/psum | solution.py:21
  16.0 1.1 fusion.11
  17.1 1.6 collective-permute-start
  18.8 7.1 %collective-permute-done = bf16[128,1024]{1,0:T(8,128)(2,1)S(1)} collective-permute-done((bf16[128,1024]{1,0:T(8,128)(2,1)S(1)}, bf16[128,1024]{1,0:T(8,128)(2,1)S(1)}, u32[]{:S(2)}, u32[]{:S(2)}) %collective-permute-start) | collective-permute-done | bytes 262176 | tf_op jit(solution)/shard_map/ppermute | solution.py:28
  25.9 0.0 collective-permute-start.1
  25.9 3.8 %collective-permute-start.2 = (bf16[128,1024]{1,0:T(8,128)(2,1)S(1)}, bf16[128,1024]{1,0:T(8,128)(2,1)S(1)}, u32[]{:S(2)}, u32[]{:S(2)}) collective-permute-start(bf16[128,1024]{1,0:T(8,128)(2,1)S(1)} %fusion.11), channel_id=1, source_target_pairs={{0,12},{4,0},{8,4},{12,8},{1,13},{5,1},{9,5},{13,9},{2,14},{6,2},{... | collective-permute-start | bytes 786440 | tf_op jit(solution)/shard_map/ppermute | solution.py:30
  29.7 6.9 %collective-permute-done.1 = bf16[128,1024]{1,0:T(8,128)(2,1)S(1)} collective-permute-done((bf16[128,1024]{1,0:T(8,128)(2,1)S(1)}, bf16[128,1024]{1,0:T(8,128)(2,1)S(1)}, u32[]{:S(2)}, u32[]{:S(2)}) %collective-permute-start.1) | collective-permute-done | bytes 262176 | tf_op jit(solution)/shard_map/ppermute | solution.py:28
  36.6 1.1 constant_dynamic-update-slice_fusion.5
  37.7 0.0 collective-permute-done.2
  37.8 0.0 copy-done
  37.8 0.0 copy-done.1
  37.8 0.1 constant_dynamic-update-slice_fusion.1
  38.0 14.6 %fusion.4 = bf16[512,8192]{1,0:T(8,128)(2,1)} fusion(bf16[1024,4096]{1,0:T(8,128)(2,1)} %param.8, bf16[1024,4096]{1,0:T(8,128)(2,1)} %param.7, bf16[1024,1024]{1,0:T(8,128)(2,1)S(1)} %constant_dynamic-update-slice_fusion, s32[]{:T(128)S(6)} %select_n.14), kind=kOutput, calls=%fused_computation.4 | convolution fusion | flops 8627683328 | bytes 26214404 | tf_op jit(solution)/shard_map/dot_general | solution.py:35
  52.6 0.0 reduce-scatter.3.cloned.1.call-update
  52.6 0.0 all-gather.2.cloned.1.call-start
  52.7 72.7 %reduce-scatter.3.cloned.1.call-done = bf16[128,8192]{1,0:T(8,128)(2,1)} async-done(((bf16[512,8192]{1,0:T(8,128)(2,1)}), bf16[128,8192]{1,0:T(8,128)(2,1)}) %reduce-scatter.3.cloned.1.call-update) | async-done | bytes 2097168 | tf_op jit(solution)/shard_map/reduce_scatter | solution.py:34
  125.4 2.0 convert_element_type.22
  127.4 1.6 fusion.7
  128.9 0.0 all-gather.2.cloned.1.call-update
  129.0 0.0 reduce-scatter.5.cloned.1.call-start
  129.0 34.6 %all-gather.2.cloned.1.call-done = bf16[512,4096]{1,0:T(8,128)(2,1)} async-done(((bf16[128,4096]{1,0:T(8,128)(2,1)}), bf16[512,4096]{1,0:T(8,128)(2,1)}) %all-gather.2.cloned.1.call-update) | async-done | bytes 4194320 | tf_op jit(solution)/shard_map/all_gather | solution.py:41
  163.6 10.1 %convolution_convert_fusion = bf16[512,1024]{1,0:T(8,128)(2,1)} fusion(bf16[512,4096]{1,0:T(8,128)(2,1)} %all-gather.2.cloned.1.call-done, bf16[4096,1024]{1,0:T(8,128)(2,1)} %param.9), kind=kOutput, calls=%fused_computation.7 | convolution fusion | flops 4295491584 | bytes 13631488 | tf_op jit(solution)/shard_map/dot_general | solution.py:44
  173.7 0.0 reduce-scatter.5.cloned.1.call-update
  173.8 27.3 %reduce-scatter.5.cloned.1.call-done = bf16[128,1024]{1,0:T(8,128)(2,1)} async-done(((bf16[512,1024]{1,0:T(8,128)(2,1)}), bf16[128,1024]{1,0:T(8,128)(2,1)}) %reduce-scatter.5.cloned.1.call-update) | async-done | bytes 262160 | tf_op jit(solution)/shard_map/reduce_scatter | solution.py:43
  (7 shorter events, 0.1 us)
Async XLA Ops:
  6.5 31.3 %copy-start = (bf16[128,1024]{1,0:T(8,128)(2,1)S(1)}, bf16[128,1024]{1,0:T(8,128)(2,1)}, u32[]{:S(2)}) copy-start(bf16[128,1024]{1,0:T(8,128)(2,1)} %param.5) | copy-start | bytes 786436
  6.5 31.3 %copy-start.1 = (f32[1024]{0:T(1024)S(1)}, f32[1024]{0:T(1024)}, u32[]{:S(2)}) copy-start(f32[1024]{0:T(1024)} %param.6) | copy-start | bytes 12292
  6.5 118.8 %reduce-scatter.3.cloned.1.call-start = ((), (), s32[]{:S(2)}) async-start(), calls=%async_computation.2 | async-start | bytes 10485760 | tf_op jit(solution)/shard_map/reduce_scatter | solution.py:34
  17.1 8.8 %collective-permute-start = (bf16[128,1024]{1,0:T(8,128)(2,1)S(1)}, bf16[128,1024]{1,0:T(8,128)(2,1)S(1)}, u32[]{:S(2)}, u32[]{:S(2)}) collective-permute-start(bf16[128,1024]{1,0:T(8,128)(2,1)S(1)} %fusion.11), channel_id=1, source_target_pairs={{0,4},{4,8},{8,12},{12,0},{1,5},{5,9},{9,13},{13,1},{2,6},{6,10},{... | collective-permute-start | bytes 786440 | tf_op jit(solution)/shard_map/ppermute | solution.py:28
  25.9 10.7 %collective-permute-start.1 = (bf16[128,1024]{1,0:T(8,128)(2,1)S(1)}, bf16[128,1024]{1,0:T(8,128)(2,1)S(1)}, u32[]{:S(2)}, u32[]{:S(2)}) collective-permute-start(bf16[128,1024]{1,0:T(8,128)(2,1)S(1)} %collective-permute-done), channel_id=1, source_target_pairs={{0,4},{4,8},{8,12},{12,0},{1,5},{5,9},{9,13},{13,1},{2,6},{6,10},{... | collective-permute-start | bytes 786440 | tf_op jit(solution)/shard_map/ppermute | solution.py:28
  25.9 11.8 %collective-permute-start.2 = (bf16[128,1024]{1,0:T(8,128)(2,1)S(1)}, bf16[128,1024]{1,0:T(8,128)(2,1)S(1)}, u32[]{:S(2)}, u32[]{:S(2)}) collective-permute-start(bf16[128,1024]{1,0:T(8,128)(2,1)S(1)} %fusion.11), channel_id=1, source_target_pairs={{0,12},{4,0},{8,4},{12,8},{1,13},{5,1},{9,5},{13,9},{2,14},{6,2},{... | collective-permute-start | bytes 786440 | tf_op jit(solution)/shard_map/ppermute | solution.py:30
  52.6 111.0 %all-gather.2.cloned.1.call-start = ((), (), s32[]{:S(2)}) async-start(), calls=%async_computation.3 | async-start | bytes 5242880 | tf_op jit(solution)/shard_map/all_gather | solution.py:41
  129.0 72.1 %reduce-scatter.5.cloned.1.call-start = ((), (), s32[]{:S(2)}) async-start(), calls=%async_computation.4 | async-start | bytes 1310720 | tf_op jit(solution)/shard_map/reduce_scatter | solution.py:43
Sparse Core Ops, SparseCore 0:
  52.7 72.6 reduce-scatter.2
  129.1 34.4 all-gather.1
  173.9 27.1 reduce-scatter.4
